TPU v7x, 32 devices: a whole 2x2x4 slice. The times are simulated.
32 devices in a mesh: groups: 1, rows: 16 (over z, y, x), cols: 2 (over core).
Axes of the slice: x: 2, y: 2, z: 4, core: 2. Of those that a mesh axis runs over, the one named last changes fastest.
Arguments:
- pool_acts: bfloat16 [6144, 1536], P(('groups', 'rows'), 'cols'), may hold values from -1 to 1
- pool_grads: bfloat16 [6144, 4096], P(('groups', 'rows'), 'cols'), may hold values from -0.75 to 0.75
- label_acts: bfloat16 [256, 1536], P(('groups', 'rows'), 'cols'), may hold values from -1 to 1
- label_grads: bfloat16 [256, 4096], P(('groups', 'rows'), 'cols'), may hold values from -0.75 to 0.75
Outputs:
- ntk: float32 [6144, 2, 128], P(('groups', 'rows'), 'cols')
All inputs are finite; a program needn't handle non-finite values.
Results may differ from a plain program's by a relative error of at most 0.0003.
Values may be sent and summed in bfloat16 or wider, within the bound.
A program may use at most 64 MiB of HBM per device.

v0:
```python
import jax
import jax.numpy as jnp
from jax import lax
from jax.sharding import PartitionSpec as P


def contract(left, right):
    return lax.dot_general(
        left, right, (((1,), (1,)), ((), ())), preferred_element_type=jnp.float32
    )


def body(pool_acts, pool_grads, label_acts, label_grads):
    own_width = pool_acts.shape[1]
    pool_rows = pool_acts.shape[0]
    joined = jnp.concatenate([label_acts, label_grads], axis=1)
    rows_in = lax.all_gather(joined, "rows", axis=0, tiled=True)
    acts_gram = contract(pool_acts, rows_in[:, :own_width])
    grad_gram = contract(pool_grads, rows_in[:, own_width:])
    partial_grams = jnp.stack([acts_gram, grad_gram])
    col_count = lax.axis_size("cols")
    blocks = lax.axis_size("rows")
    half_len = partial_grams.shape[2] // blocks // col_count
    partial_grams = partial_grams.reshape(2, pool_rows, blocks, col_count, half_len)
    partial_grams = jnp.transpose(partial_grams, (0, 1, 3, 2, 4))
    partial_grams = partial_grams.reshape(2, pool_rows, col_count, blocks * half_len)
    summed = lax.psum_scatter(partial_grams, "cols", scatter_dimension=2, tiled=True)
    return summed[0] * summed[1]


def solution(mesh):
    placed = (
        P(("groups", "rows"), "cols"),
        P(("groups", "rows"), "cols"),
        P(("groups", "rows"), "cols"),
        P(("groups", "rows"), "cols"),
    )
    return jax.shard_map(
        body,
        mesh=mesh,
        in_specs=placed,
        out_specs=P(("groups", "rows"), "cols", None),
        check_vma=False,
    )
```

profile of v0, /device:TPU:9, one launch (start us, length us, event | category | flops | bytes accessed | tf_op | source)
XLA Modules:
  0.0 101.2 jit_solution(12916475489620022041)
XLA Ops:
  6.5 0.0 copy-start
  6.5 0.0 all-gather.2.cloned.1.call-start
  6.5 1.6 %pad_maximum_fusion.1 = bf16[16,2816]{1,0:T(8,128)(2,1)} fusion(bf16[16,2048]{1,0:T(8,128)(2,1)} %param.7, bf16[16,768]{1,0:T(8,128)(2,1)} %param.6), kind=kLoop, calls=%fused_computation.8 | loop fusion | flops 180224 | bytes 180224 | tf_op jit(solution)/shard_map/concatenate | solution.py:16
  8.1 0.0 all-gather.2.cloned.1.call-update
  8.2 0.0 all-reduce.3.cloned.1.call-start
  8.2 58.6 %all-gather.2.cloned.1.call-done = bf16[256,2816]{1,0:T(8,128)(2,1)} async-done(((bf16[16,2816]{1,0:T(8,128)(2,1)}), bf16[256,2816]{1,0:T(8,128)(2,1)}) %all-gather.2.cloned.1.call-update) | async-done | bytes 1441808 | tf_op jit(solution)/shard_map/all_gather | solution.py:17
  66.8 1.6 %fusion.2 = f32[256,384]{1,0:T(8,128)S(1)} fusion(bf16[384,768]{1,0:T(8,128)(2,1)} %param.4, bf16[256,2816]{1,0:T(8,128)(2,1)} %all-gather.2.cloned.1.call-done), kind=kOutput, calls=%fused_computation.4 | convolution fusion | flops 150994944 | bytes 1376256 | tf_op jit(solution)/shard_map/dot_general | solution.py:8
  68.4 0.0 copy-done
  68.4 1.9 %fusion = f32[256,384]{1,0:T(8,128)S(1)} fusion(bf16[384,2048]{1,0:T(8,128)(2,1)S(1)} %copy-done, bf16[256,2816]{1,0:T(8,128)(2,1)} %all-gather.2.cloned.1.call-done), kind=kOutput, calls=%fused_computation | convolution fusion | flops 402653184 | bytes 3014656 | tf_op jit(solution)/shard_map/dot_general | solution.py:8
  70.3 0.0 copy-start.1
  70.4 0.9 copy_bitcast_fusion
  71.3 0.0 all-reduce.3.cloned.1.call-update
  71.3 0.0 copy-done.1
  71.3 0.6 dynamic-slice
  71.9 20.0 %all-reduce.3.cloned.1.call-done = f32[2,384,2,128]{1,3,2,0:T(8,128)} async-done(((f32[2,384,2,128]{1,3,2,0:T(8,128)}), f32[2,384,2,128]{1,3,2,0:T(8,128)}) %all-reduce.3.cloned.1.call-update) | async-done | bytes 786448
  91.9 1.7 %fusion.4 = f32[384,1,128]{0,2,1:T(8,128)S(1)} fusion(f32[2,384,2,128]{1,3,2,0:T(8,128)} %all-reduce.3.cloned.1.call-done, u32[]{:T(128)S(6)} %convert, u32[]{:T(128)} %bitcast.18), kind=kLoop, calls=%fused_computation.7 | loop fusion | flops 49152 | bytes 589832 | tf_op jit(solution)/shard_map/mul | solution.py:28
  93.6 0.8 copy.11
Async XLA Ops:
  6.5 61.8 %copy-start = (bf16[384,2048]{1,0:T(8,128)(2,1)S(1)}, bf16[384,2048]{1,0:T(8,128)(2,1)}, u32[]{:S(2)}) copy-start(bf16[384,2048]{1,0:T(8,128)(2,1)} %param.5) | copy-start | bytes 4718596
  6.5 60.3 %all-gather.2.cloned.1.call-start = ((), (), s32[]{:S(2)}) async-start(), calls=%async_computation | async-start | bytes 1531904 | tf_op jit(solution)/shard_map/all_gather | solution.py:17
  8.2 83.7 %all-reduce.3.cloned.1.call-start = ((), (), s32[]{:S(2)}) async-start(), calls=%async_computation.1 | async-start | bytes 1572864
  70.3 1.0 copy-start.1
Sparse Core Ops, SparseCore 0:
  10.0 56.7 all-gather.1
  71.4 20.4 all-reduce.2
where the time goes:
time: 102 us; the launch traced here: 101 us
  waiting for transfers between devices  78.6 us (77%)
  between operations  13.4 us (13%)
  other arithmetic  4.24 us (4%)
  matrix products  3.51 us (3%)
  local copies, waits for them, and re-layouts  1.41 us (1%)
    all_gather x1, waiting for transfers between devices, body(): rows_in = lax.all_gather(joined, 'rows', axis=0, tiled=True)  58.6 us
    unnamed x3, waiting for transfers between devices  20 us
    dot_general x2, matrix products, contract(): lax.dot_general(left, right, (((1,), (1,)), ((), ())), preferred_element_...  3.51 us
  transfers between devices with their start and end apart: 2, of which 2 were waited for; matrix products, arithmetic and copies ran while one was open for 1% of the time, Pallas kernels for 0%

commit v1 on v0

v1 whole, which is shorter than its diff:
```python
import functools

import jax
import jax.numpy as jnp
from jax import lax
from jax.experimental import pallas as pl
from jax.experimental.pallas import tpu as pltpu
from jax.sharding import PartitionSpec as P

MESH = pl.DeviceIdType.MESH
ORDERS = ((0, 2, 1), (0, 1, 2), (2, 0, 1), (1, 0, 2))
LANES = 128


def contract(left, right):
    return lax.dot_general(
        left, right, (((1,), (1,)), ((), ())), preferred_element_type=jnp.float32
    )


def kernel(
    sizes, spans,
    pool_acts, pool_grads, label_acts, label_grads, out_ref,
    buf0, buf1, buf2, buf3, acts, grads, gram, other,
    send_sem, recv_sem, local_sem, pair_send, pair_recv,
):
    bufs = (buf0, buf1, buf2, buf3)
    me = lax.axis_index("rows")
    core = lax.axis_index("cols")
    strides = (sizes[1] * sizes[2], sizes[2], 1)
    place = [lax.rem(me // s, n) for s, n in zip(strides, sizes)]
    blocks = sizes[0] * sizes[1] * sizes[2]

    def at(delta):
        return sum(
            lax.rem(place[a] + delta[a], sizes[a]) * strides[a] for a in range(3)
        )

    def along(axis):
        return [
            tuple(d if a == axis else 0 for a in range(3))
            for d in range(1, sizes[axis])
        ]

    barrier = pltpu.get_barrier_semaphore()
    greeted = 1
    pl.semaphore_signal(
        barrier, inc=1, device_id={"cols": 1 - core}, device_id_type=MESH
    )
    for axis in range(3):
        for peer in along(axis):
            pl.semaphore_signal(
                barrier, inc=1, device_id={"rows": at(peer)}, device_id_type=MESH
            )
            greeted += 1
    pl.semaphore_wait(barrier, greeted)

    own = [label_acts if s is None else label_grads.at[:, s[0] : s[1]] for s in spans]
    sent = []

    def send(k, delta, peer):
        block = at(delta)
        src = bufs[k].at[block] if any(delta) else own[k]
        copy = pltpu.make_async_remote_copy(
            src_ref=src,
            dst_ref=bufs[k].at[block],
            send_sem=send_sem.at[len(sent)],
            recv_sem=recv_sem.at[k, block],
            device_id={"rows": at(peer)},
            device_id_type=MESH,
        )
        copy.start()
        sent.append(copy)

    def arrived(k, delta):
        block = at(delta)
        pltpu.make_async_remote_copy(
            src_ref=bufs[k].at[block],
            dst_ref=bufs[k].at[block],
            send_sem=send_sem.at[0],
            recv_sem=recv_sem.at[k, block],
            device_id={"rows": at(along(2)[0])},
            device_id_type=MESH,
        ).wait_recv()

    def plus(*deltas):
        return tuple(sum(d) for d in zip(*deltas))

    zero = (0, 0, 0)
    for leg in range(3):
        for k, order in enumerate(ORDERS):
            for peer in along(order[leg]):
                send(k, zero, peer)

    local = [
        pltpu.make_async_copy(own[k], bufs[k].at[me], local_sem.at[k])
        for k in range(4)
    ]
    local.append(pltpu.make_async_copy(pool_acts, acts, local_sem.at[4]))
    local.append(pltpu.make_async_copy(pool_grads, grads, local_sem.at[5]))
    for copy in local:
        copy.start()

    for step in range(max(sizes) - 1):
        for k, order in enumerate(ORDERS):
            first = along(order[0])
            if step < len(first):
                arrived(k, first[step])
                for leg in (1, 2):
                    for peer in along(order[leg]):
                        send(k, first[step], peer)

    second = [
        [plus(f, s) for f in [zero] + along(o[0]) for s in along(o[1])]
        for o in ORDERS
    ]
    for step in range(max(len(s) for s in second)):
        for k, order in enumerate(ORDERS):
            if step < len(second[k]):
                arrived(k, second[k][step])
                for peer in along(order[2]):
                    send(k, second[k][step], peer)

    third = [
        [
            plus(f, s, t)
            for f in [zero] + along(o[0])
            for s in [zero] + along(o[1])
            for t in along(o[2])
        ]
        for o in ORDERS
    ]

    def pair(which):
        return pltpu.make_async_remote_copy(
            src_ref=gram.at[which, :, 1 - core],
            dst_ref=other.at[which],
            send_sem=pair_send.at[which],
            recv_sem=pair_recv.at[which],
            device_id={"cols": 1 - core},
            device_id_type=MESH,
        )

    def flat(k):
        return bufs[k][...].reshape(blocks * bufs[k].shape[1], bufs[k].shape[2])

    for copy in local:
        copy.wait()
    for delta in third[0]:
        arrived(0, delta)
    gram[0] = contract(flat(0), acts[...]).reshape(gram.shape[1:])
    pair(0).start()
    for k in (1, 2, 3):
        for delta in third[k]:
            arrived(k, delta)
    total = None
    for k in (1, 2, 3):
        part = contract(flat(k), grads[:, spans[k][0] : spans[k][1]])
        total = part if total is None else total + part
    gram[1] = total.reshape(gram.shape[1:])
    pair(1).start()
    pair(0).wait()
    pair(1).wait()
    result = (gram[0, :, core] + other[0]) * (gram[1, :, core] + other[1])
    out_ref[...] = result.reshape(out_ref.shape[1], out_ref.shape[0]).T
    for copy in sent:
        copy.wait_send()


def body(pool_acts, pool_grads, label_acts, label_grads):
    blocks = lax.axis_size("rows")
    cols = lax.axis_size("cols")
    sizes = (blocks // 4, 2, 2)
    pool_rows = pool_acts.shape[0]
    block_rows = label_acts.shape[0]
    half = block_rows // cols
    wide = label_grads.shape[1]
    quarter = wide // 4
    spans = (None, (0, 2 * quarter), (2 * quarter, 3 * quarter), (3 * quarter, wide))
    widths = (label_acts.shape[1], 2 * quarter, quarter, wide - 3 * quarter)
    sends = 0
    for o in ORDERS:
        n = [sizes[a] for a in o]
        sends += (n[0] - 1) + n[0] * (n[1] - 1) + n[0] * n[1] * (n[2] - 1)
    out = pl.pallas_call(
        functools.partial(kernel, sizes, spans),
        out_shape=jax.ShapeDtypeStruct((pool_rows, blocks * half), jnp.float32),
        in_specs=[pl.BlockSpec(memory_space=pltpu.HBM)] * 4,
        out_specs=pl.BlockSpec(memory_space=pltpu.VMEM),
        scratch_shapes=[
            pltpu.VMEM((blocks, block_rows, w), jnp.bfloat16) for w in widths
        ]
        + [
            pltpu.VMEM(pool_acts.shape, jnp.bfloat16),
            pltpu.VMEM(pool_grads.shape, jnp.bfloat16),
            pltpu.VMEM((2, blocks, cols, half, pool_rows), jnp.float32),
            pltpu.VMEM((2, blocks, half, pool_rows), jnp.float32),
            pltpu.SemaphoreType.DMA((sends,)),
            pltpu.SemaphoreType.DMA((4, blocks)),
            pltpu.SemaphoreType.DMA((6,)),
            pltpu.SemaphoreType.DMA((2,)),
            pltpu.SemaphoreType.DMA((2,)),
        ],
        compiler_params=pltpu.CompilerParams(
            collective_id=0, has_side_effects=True, vmem_limit_bytes=48 * 2**20
        ),
    )(pool_acts, pool_grads, label_acts, label_grads)
    return out.reshape(pool_rows, 1, blocks * half)


def solution(mesh):
    placed = (
        P(("groups", "rows"), "cols"),
        P(("groups", "rows"), "cols"),
        P(("groups", "rows"), "cols"),
        P(("groups", "rows"), "cols"),
    )
    return jax.shard_map(
        body,
        mesh=mesh,
        in_specs=placed,
        out_specs=P(("groups", "rows"), "cols", None),
        check_vma=False,
    )
```

time: 102 us -> 30 us (0.29)
  waiting for transfers between devices: 78.6 us -> 0 us
  Pallas kernels: 0 us -> 25 us
  between operations: 13.4 us -> 0.01 us
  other arithmetic: 4.24 us -> 0 us
  matrix products: 3.51 us -> 0 us
  local copies, waits for them, and re-layouts: 1.41 us -> 4.73 us
    all_gather x1 -> x0, waiting for transfers between devices: 58.6 us -> none  [body(): rows_in = lax.all_gather(joined, 'rows', axis=0, tiled=True)]
    pallas_call x0 -> x1, Pallas kernels: none -> 25 us  [body(): pl.pallas_call(functools.partial(kernel, sizes, spans), out_shape=jax.Sha...]
    unnamed x3 -> x0, waiting for transfers between devices: 20 us -> none
    unnamed x5 -> x9, local copies, waits for them, and re-layouts: 0.6 us -> 4.73 us
    dot_general x2 -> x0, matrix products: 3.51 us -> none  [contract(): lax.dot_general(left, right, (((1,), (1,)), ((), ())), preferred_element_...]
    mul x1 -> x0, other arithmetic: 1.69 us -> none  [body(): return summed[0] * summed[1]]
    concatenate x1 -> x0, other arithmetic: 1.6 us -> none  [body(): joined = jnp.concatenate([label_acts, label_grads], axis=1)]
  transfers between devices with their start and end apart: 2 -> 0, of which waited for: 2 -> 0; matrix products, arithmetic and copies ran while one was open for 1% -> 0% of each run, Pallas kernels for 0% -> 0%
where the time goes in v1:
time: 30 us; the launch traced here: 29.7 us
  Pallas kernels  25 us (83%)
  local copies, waits for them, and re-layouts  4.73 us (16%)
    pallas_call x1, Pallas kernels, body(): pl.pallas_call(functools.partial(kernel, sizes, spans), out_shape=jax.Sha...  25 us
    unnamed x9, local copies, waits for them, and re-layouts  4.73 us

profile of v1, /device:TPU:9, one launch (start us, length us, event | category | flops | bytes accessed | tf_op | source)
XLA Modules:
  0.0 29.7 jit_solution(14949556409382649910)
XLA Ops:
  0.0 0.0 copy-start
  0.0 1.4 %copy-done = bf16[384,2048]{1,0:T(8,128)(2,1)S(1)} copy-done((bf16[384,2048]{1,0:T(8,128)(2,1)S(1)}, bf16[384,2048]{1,0:T(8,128)(2,1)}, u32[]{:S(2)}) %copy-start) | copy-done | bytes 1572888
  1.4 0.0 copy-start.1
  1.4 1.1 %copy-done.1 = bf16[384,768]{1,0:T(8,128)(2,1)S(1)} copy-done((bf16[384,768]{1,0:T(8,128)(2,1)S(1)}, bf16[384,768]{1,0:T(8,128)(2,1)}, u32[]{:S(2)}) %copy-start.1) | copy-done | bytes 589848
  2.5 0.0 copy-start.2
  2.5 0.8 %copy-done.2 = bf16[16,2048]{1,0:T(8,128)(2,1)S(1)} copy-done((bf16[16,2048]{1,0:T(8,128)(2,1)S(1)}, bf16[16,2048]{1,0:T(8,128)(2,1)}, u32[]{:S(2)}) %copy-start.2) | copy-done | bytes 65560
  3.3 0.0 copy-start.3
  3.3 0.7 %copy-done.3 = bf16[16,768]{1,0:T(8,128)(2,1)S(1)} copy-done((bf16[16,768]{1,0:T(8,128)(2,1)S(1)}, bf16[16,768]{1,0:T(8,128)(2,1)}, u32[]{:S(2)}) %copy-start.3) | copy-done | bytes 24600
  4.1 25.0 %shard_map.46 = f32[384,128]{1,0:T(8,128)S(1)} custom-call(bf16[384,768]{1,0:T(8,128)(2,1)S(1)} %copy-done.1, bf16[384,2048]{1,0:T(8,128)(2,1)S(1)} %copy-done, bf16[16,768]{1,0:T(8,128)(2,1)S(1)} %copy-done.3, bf16[16,2048]{1,0:T(8,128)(2,1)S(1)} %copy-done.2), custom_call_target="tpu_custom_call" | custom-call | tf_op jit(solution)/shard_map/pallas_call | solution.py:185
  29.1 0.7 %copy.7 = f32[384,1,128]{2,1,0:T(1,128)} copy(f32[384,1,128]{2,1,0:T(1,128)S(1)} %bitcast.3) | data formatting | bytes 393216
Async XLA Ops:
  0.0 1.4 %copy-start = (bf16[384,2048]{1,0:T(8,128)(2,1)S(1)}, bf16[384,2048]{1,0:T(8,128)(2,1)}, u32[]{:S(2)}) copy-start(bf16[384,2048]{1,0:T(8,128)(2,1)} %pool_grads.1) | copy-start | bytes 4718596
  1.4 1.1 %copy-start.1 = (bf16[384,768]{1,0:T(8,128)(2,1)S(1)}, bf16[384,768]{1,0:T(8,128)(2,1)}, u32[]{:S(2)}) copy-start(bf16[384,768]{1,0:T(8,128)(2,1)} %pool_acts.1) | copy-start | bytes 1769476
  2.5 0.8 %copy-start.2 = (bf16[16,2048]{1,0:T(8,128)(2,1)S(1)}, bf16[16,2048]{1,0:T(8,128)(2,1)}, u32[]{:S(2)}) copy-start(bf16[16,2048]{1,0:T(8,128)(2,1)} %label_grads.1) | copy-start | bytes 196612
  3.3 0.7 %copy-start.3 = (bf16[16,768]{1,0:T(8,128)(2,1)S(1)}, bf16[16,768]{1,0:T(8,128)(2,1)}, u32[]{:S(2)}) copy-start(bf16[16,768]{1,0:T(8,128)(2,1)} %label_acts.1) | copy-start | bytes 73732

commit v2 on v1

--- a/solution.py
+++ b/solution.py
@@ -202,7 +202,7 @@
             pltpu.SemaphoreType.DMA((2,)),
         ],
         compiler_params=pltpu.CompilerParams(
-            collective_id=0, has_side_effects=True, vmem_limit_bytes=48 * 2**20
+            collective_id=0, has_side_effects=True, vmem_limit_bytes=63 * 2**20
         ),
     )(pool_acts, pool_grads, label_acts, label_grads)
     return out.reshape(pool_rows, 1, blocks * half)

time: 30 us -> 27.7 us (0.923)
  local copies, waits for them, and re-layouts: 4.73 us -> 1.62 us
  Pallas kernels: 25 us -> 25.9 us
    unnamed x9 -> x1, local copies, waits for them, and re-layouts: 4.73 us -> 1.62 us
    pallas_call x1, Pallas kernels: 25 us -> 25.9 us  [body(): pl.pallas_call(functools.partial(kernel, sizes, spans), out_shape=jax.Sha...]
where the time goes in v2:
time: 27.7 us; the launch traced here: 27.5 us
  Pallas kernels  25.9 us (94%)
  local copies, waits for them, and re-layouts  1.62 us (6%)
    pallas_call x1, Pallas kernels, body(): pl.pallas_call(functools.partial(kernel, sizes, spans), out_shape=jax.Sha...  25.9 us
    unnamed x1, local copies, waits for them, and re-layouts  1.62 us

profile of v2, /device:TPU:9, one launch (start us, length us, event | category | flops | bytes accessed | tf_op | source)
XLA Modules:
  0.0 27.5 jit_solution(4192694065748631430)
XLA Ops:
  0.0 25.9 %shard_map.46 = f32[384,128]{1,0:T(8,128)} custom-call(bf16[384,768]{1,0:T(8,128)(2,1)} %pool_acts.1, bf16[384,2048]{1,0:T(8,128)(2,1)} %pool_grads.1, bf16[16,768]{1,0:T(8,128)(2,1)} %label_acts.1, bf16[16,2048]{1,0:T(8,128)(2,1)} %label_grads.1), custom_call_target="tpu_custom_call" | custom-call | tf_op jit(solution)/shard_map/pallas_call | solution.py:185
  25.9 1.6 %copy.7 = f32[384,1,128]{2,1,0:T(1,128)} copy(f32[384,1,128]{2,1,0:T(1,128)} %bitcast.3) | data formatting | bytes 393216

commit v3 on v2

--- a/solution.py
+++ b/solution.py
@@ -31,16 +31,31 @@
     place = [lax.rem(me // s, n) for s, n in zip(strides, sizes)]
     blocks = sizes[0] * sizes[1] * sizes[2]
 
+    def flip(value, bits):
+        out, bit = 0, 1
+        while bit < max(sizes):
+            out += lax.rem(value // bit + bits // bit, 2) * bit
+            bit *= 2
+        return out
+
     def at(delta):
-        return sum(
-            lax.rem(place[a] + delta[a], sizes[a]) * strides[a] for a in range(3)
-        )
+        return sum(flip(place[a], delta[a]) * strides[a] for a in range(3))
 
     def along(axis):
         return [
             tuple(d if a == axis else 0 for a in range(3))
             for d in range(1, sizes[axis])
         ]
+
+    own = [label_acts if s is None else label_grads.at[:, s[0] : s[1]] for s in spans]
+    local = [
+        pltpu.make_async_copy(own[k], bufs[k].at[me], local_sem.at[k])
+        for k in range(4)
+    ]
+    local.append(pltpu.make_async_copy(pool_acts, acts, local_sem.at[4]))
+    local.append(pltpu.make_async_copy(pool_grads, grads, local_sem.at[5]))
+    for copy in local:
+        copy.start()
 
     barrier = pltpu.get_barrier_semaphore()
     greeted = 1
@@ -54,15 +69,15 @@
             )
             greeted += 1
     pl.semaphore_wait(barrier, greeted)
-
-    own = [label_acts if s is None else label_grads.at[:, s[0] : s[1]] for s in spans]
+    for copy in local[:4]:
+        copy.wait()
+
     sent = []
 
     def send(k, delta, peer):
         block = at(delta)
-        src = bufs[k].at[block] if any(delta) else own[k]
         copy = pltpu.make_async_remote_copy(
-            src_ref=src,
+            src_ref=bufs[k].at[block],
             dst_ref=bufs[k].at[block],
             send_sem=send_sem.at[len(sent)],
             recv_sem=recv_sem.at[k, block],
@@ -84,7 +99,7 @@
         ).wait_recv()
 
     def plus(*deltas):
-        return tuple(sum(d) for d in zip(*deltas))
+        return tuple(functools.reduce(lambda p, q: p ^ q, d) for d in zip(*deltas))
 
     zero = (0, 0, 0)
     for leg in range(3):
@@ -92,34 +107,19 @@
             for peer in along(order[leg]):
                 send(k, zero, peer)
 
-    local = [
-        pltpu.make_async_copy(own[k], bufs[k].at[me], local_sem.at[k])
-        for k in range(4)
-    ]
-    local.append(pltpu.make_async_copy(pool_acts, acts, local_sem.at[4]))
-    local.append(pltpu.make_async_copy(pool_grads, grads, local_sem.at[5]))
-    for copy in local:
-        copy.start()
-
-    for step in range(max(sizes) - 1):
-        for k, order in enumerate(ORDERS):
-            first = along(order[0])
-            if step < len(first):
-                arrived(k, first[step])
-                for leg in (1, 2):
-                    for peer in along(order[leg]):
-                        send(k, first[step], peer)
-
-    second = [
-        [plus(f, s) for f in [zero] + along(o[0]) for s in along(o[1])]
-        for o in ORDERS
-    ]
-    for step in range(max(len(s) for s in second)):
-        for k, order in enumerate(ORDERS):
-            if step < len(second[k]):
-                arrived(k, second[k][step])
-                for peer in along(order[2]):
-                    send(k, second[k][step], peer)
+    passed = []
+    for k, order in enumerate(ORDERS):
+        for f in [zero] + along(order[0]):
+            if any(f):
+                passed.append((k, f, (1, 2)))
+            for s in along(order[1]):
+                passed.append((k, plus(f, s), (2,)))
+    passed.sort(key=lambda e: ((-len(e[2]), sum(d.bit_length() for d in e[1]))))
+    for k, delta, legs in passed:
+        arrived(k, delta)
+        for leg in legs:
+            for peer in along(ORDERS[k][leg]):
+                send(k, delta, peer)
 
     third = [
         [
@@ -144,7 +144,7 @@
     def flat(k):
         return bufs[k][...].reshape(blocks * bufs[k].shape[1], bufs[k].shape[2])
 
-    for copy in local:
+    for copy in local[4:]:
         copy.wait()
     for delta in third[0]:
         arrived(0, delta)

time: 27.7 us -> 26 us (0.939)
  the two profiles are of different devices: /device:TPU:9 before, /device:TPU:0 now
where the time goes in v3:
time: 26 us; the launch traced here: 25.8 us
  Pallas kernels  24.2 us (93%)
  local copies, waits for them, and re-layouts  1.62 us (6%)
    pallas_call x1, Pallas kernels, body(): pl.pallas_call(functools.partial(kernel, sizes, spans), out_shape=jax.Sha...  24.2 us
    unnamed x1, local copies, waits for them, and re-layouts  1.62 us

profile of v3, /device:TPU:0, one launch (start us, length us, event | category | flops | bytes accessed | tf_op | source)
XLA Modules:
  0.0 25.8 jit_solution(6085182892318537338)
XLA Ops:
  0.0 24.2 %shard_map.46 = f32[384,128]{1,0:T(8,128)} custom-call(bf16[384,768]{1,0:T(8,128)(2,1)} %pool_acts.1, bf16[384,2048]{1,0:T(8,128)(2,1)} %pool_grads.1, bf16[16,768]{1,0:T(8,128)(2,1)} %label_acts.1, bf16[16,2048]{1,0:T(8,128)(2,1)} %label_grads.1), custom_call_target="tpu_custom_call" | custom-call | tf_op jit(solution)/shard_map/pallas_call | solution.py:185
  24.2 1.6 %copy.7 = f32[384,1,128]{2,1,0:T(1,128)} copy(f32[384,1,128]{2,1,0:T(1,128)} %bitcast.3) | data formatting | bytes 393216

commit v4 on v3

--- a/solution.py
+++ b/solution.py
@@ -38,8 +38,11 @@
             bit *= 2
         return out
 
+    def spot(delta):
+        return tuple(flip(place[a], delta[a]) for a in range(3))
+
     def at(delta):
-        return sum(flip(place[a], delta[a]) * strides[a] for a in range(3))
+        return sum(p * s for p, s in zip(spot(delta), strides))
 
     def along(axis):
         return [
@@ -49,7 +52,7 @@
 
     own = [label_acts if s is None else label_grads.at[:, s[0] : s[1]] for s in spans]
     local = [
-        pltpu.make_async_copy(own[k], bufs[k].at[me], local_sem.at[k])
+        pltpu.make_async_copy(own[k], bufs[k].at[tuple(place)], local_sem.at[k])
         for k in range(4)
     ]
     local.append(pltpu.make_async_copy(pool_acts, acts, local_sem.at[4]))
@@ -57,6 +60,7 @@
     for copy in local:
         copy.start()
 
+    gram[...] = jnp.zeros_like(gram)
     barrier = pltpu.get_barrier_semaphore()
     greeted = 1
     pl.semaphore_signal(
@@ -77,8 +81,8 @@
     def send(k, delta, peer):
         block = at(delta)
         copy = pltpu.make_async_remote_copy(
-            src_ref=bufs[k].at[block],
-            dst_ref=bufs[k].at[block],
+            src_ref=bufs[k].at[spot(delta)],
+            dst_ref=bufs[k].at[spot(delta)],
             send_sem=send_sem.at[len(sent)],
             recv_sem=recv_sem.at[k, block],
             device_id={"rows": at(peer)},
@@ -90,8 +94,8 @@
     def arrived(k, delta):
         block = at(delta)
         pltpu.make_async_remote_copy(
-            src_ref=bufs[k].at[block],
-            dst_ref=bufs[k].at[block],
+            src_ref=bufs[k].at[spot(delta)],
+            dst_ref=bufs[k].at[spot(delta)],
             send_sem=send_sem.at[0],
             recv_sem=recv_sem.at[k, block],
             device_id={"rows": at(along(2)[0])},
@@ -133,7 +137,7 @@
 
     def pair(which):
         return pltpu.make_async_remote_copy(
-            src_ref=gram.at[which, :, 1 - core],
+            src_ref=gram.at[which, :, :, :, 1 - core],
             dst_ref=other.at[which],
             send_sem=pair_send.at[which],
             recv_sem=pair_recv.at[which],
@@ -141,27 +145,31 @@
             device_id_type=MESH,
         )
 
-    def flat(k):
-        return bufs[k][...].reshape(blocks * bufs[k].shape[1], bufs[k].shape[2])
+    def add(k, late):
+        axis = ORDERS[k][2]
+        side = lax.rem(place[axis] + late, 2)
+        part = (slice(None),) * axis + (side,)
+        which, pool = (0, acts) if k == 0 else (1, grads)
+        rows = bufs[k][part]
+        rows = rows.reshape(-1, rows.shape[-1])
+        span = slice(None) if k == 0 else slice(*spans[k])
+        target = gram.at[(which,) + part]
+        target[...] += contract(rows, pool[:, span]).reshape(target.shape)
 
     for copy in local[4:]:
         copy.wait()
-    for delta in third[0]:
-        arrived(0, delta)
-    gram[0] = contract(flat(0), acts[...]).reshape(gram.shape[1:])
-    pair(0).start()
-    for k in (1, 2, 3):
+    for k in range(4):
+        add(k, 0)
+    for k in range(4):
         for delta in third[k]:
             arrived(k, delta)
-    total = None
-    for k in (1, 2, 3):
-        part = contract(flat(k), grads[:, spans[k][0] : spans[k][1]])
-        total = part if total is None else total + part
-    gram[1] = total.reshape(gram.shape[1:])
+        add(k, 1)
+        if k == 0:
+            pair(0).start()
     pair(1).start()
     pair(0).wait()
     pair(1).wait()
-    result = (gram[0, :, core] + other[0]) * (gram[1, :, core] + other[1])
+    result = (gram[0, :, :, :, core] + other[0]) * (gram[1, :, :, :, core] + other[1])
     out_ref[...] = result.reshape(out_ref.shape[1], out_ref.shape[0]).T
     for copy in sent:
         copy.wait_send()
@@ -176,8 +184,8 @@
     half = block_rows // cols
     wide = label_grads.shape[1]
     quarter = wide // 4
-    spans = (None, (0, 2 * quarter), (2 * quarter, 3 * quarter), (3 * quarter, wide))
-    widths = (label_acts.shape[1], 2 * quarter, quarter, wide - 3 * quarter)
+    spans = (None, (0, 1152), (1152, 1536), (1536, wide))
+    widths = (label_acts.shape[1], 1152, 384, 512)
     sends = 0
     for o in ORDERS:
         n = [sizes[a] for a in o]
@@ -188,13 +196,13 @@
         in_specs=[pl.BlockSpec(memory_space=pltpu.HBM)] * 4,
         out_specs=pl.BlockSpec(memory_space=pltpu.VMEM),
         scratch_shapes=[
-            pltpu.VMEM((blocks, block_rows, w), jnp.bfloat16) for w in widths
+            pltpu.VMEM((*sizes, block_rows, w), jnp.bfloat16) for w in widths
         ]
         + [
             pltpu.VMEM(pool_acts.shape, jnp.bfloat16),
             pltpu.VMEM(pool_grads.shape, jnp.bfloat16),
-            pltpu.VMEM((2, blocks, cols, half, pool_rows), jnp.float32),
-            pltpu.VMEM((2, blocks, half, pool_rows), jnp.float32),
+            pltpu.VMEM((2, *sizes, cols, half, pool_rows), jnp.float32),
+            pltpu.VMEM((2, *sizes, half, pool_rows), jnp.float32),
             pltpu.SemaphoreType.DMA((sends,)),
             pltpu.SemaphoreType.DMA((4, blocks)),
             pltpu.SemaphoreType.DMA((6,)),

time: 26 us -> 25.9 us (level)
  the two profiles are of different devices: /device:TPU:0 before, /device:TPU:9 now
where the time goes in v4:
time: 25.9 us; the launch traced here: 25.5 us
  Pallas kernels  23.9 us (92%)
  local copies, waits for them, and re-layouts  1.62 us (6%)
    pallas_call x1, Pallas kernels, body(): pl.pallas_call(functools.partial(kernel, sizes, spans), out_shape=jax.Sha...  23.9 us
    unnamed x1, local copies, waits for them, and re-layouts  1.62 us

profile of v4, /device:TPU:9, one launch (start us, length us, event | category | flops | bytes accessed | tf_op | source)
XLA Modules:
  0.0 25.5 jit_solution(9476349600394409414)
XLA Ops:
  0.0 23.9 %shard_map.46 = f32[384,128]{1,0:T(8,128)} custom-call(bf16[384,768]{1,0:T(8,128)(2,1)} %pool_acts.1, bf16[384,2048]{1,0:T(8,128)(2,1)} %pool_grads.1, bf16[16,768]{1,0:T(8,128)(2,1)} %label_acts.1, bf16[16,2048]{1,0:T(8,128)(2,1)} %label_grads.1), custom_call_target="tpu_custom_call" | custom-call | tf_op jit(solution)/shard_map/pallas_call | solution.py:193
  23.9 1.6 %copy.7 = f32[384,1,128]{2,1,0:T(1,128)} copy(f32[384,1,128]{2,1,0:T(1,128)} %bitcast.3) | data formatting | bytes 393216
